TPU v7x, 32 devices: a whole 2x2x4 slice. The times are simulated.
32 devices in a mesh: grp: 2 (over y), lon: 16 (over z, x, core).
Axes of the slice: x: 2, y: 2, z: 4, core: 2. Of those that a mesh axis runs over, the one named last changes fastest.
Arguments:
- ocean_state: float32 [4, 16, 128, 128], P(None, 'grp', 'lon'), parts along dimension 1, may hold values from -4 to 4
- ocean_mask: int32 [128, 128], P('lon'), may hold values 0 or 1
- polar_rows: int32 [8], replicated, may hold values from 112 to 127, as said below
- target_state: float32 [4, 16, 128, 128], P(None, 'grp', 'lon'), parts along dimension 1, may hold values from -6 to 6
- weight_in: float32 [64, 3], replicated, may hold values from -3.5 to 3.5
- bias_in: float32 [64], replicated, may hold values from -0.5 to 0.5
- weight_mid: float32 [64, 64], replicated, may hold values from -0.75 to 0.75
- bias_mid: float32 [64], replicated, may hold values from -0.5 to 0.5
- weight_out: float32 [3, 64], replicated, may hold values from -0.75 to 0.75
Outputs:
- final_state: float32 [4, 16, 128, 128], P(None, 'grp', 'lon'), parts along dimension 1
- middle_sensitivity: float32 [4, 16, 128, 128], P(None, 'grp', 'lon'), parts along dimension 1
- grad_weight_in: float32 [128, 3], P('grp'), parts along dimension 0
- grad_bias_in: float32 [128], P('grp'), parts along dimension 0
- grad_weight_mid: float32 [128, 64], P('grp'), parts along dimension 0
- grad_bias_mid: float32 [128], P('grp'), parts along dimension 0
- grad_weight_out: float32 [6, 64], P('grp'), parts along dimension 0
There are 2 independent parts, one for each index of `grp`. A program takes and returns all parts, laid end to end along the dimension named above; an argument that names none is the same for every part. Nothing has to cross between parts.
Inputs may be any that keep to these rules, and one draw needn't show every extreme that they name: `polar_rows`: 8 distinct rows in increasing order, the j-th being 128 - 2 * 8 + 2 j or the row after it.
All inputs are finite; a program needn't handle non-finite values. No bound on the sum of `ocean_mask` on one device may be relied on, other than what follows from the above.
Results may differ from a plain program's by a relative error of at most 0.000098.
Values sent between devices are 32-bit elements; how exact they have to be, the bound alone decides.
A program may use at most 128 MiB of HBM per device.

v0:
```python
import functools

import jax
import jax.numpy as jnp
import numpy as np
from jax import lax
from jax.experimental import pallas as pl
from jax.experimental.pallas import tpu as pltpu
from jax.sharding import PartitionSpec as P

DT = 0.2
VISC = 0.05
PRESS = 0.3
GAIN = 0.3
F32 = jnp.float32
BF16 = jnp.bfloat16
MESH = pl.DeviceIdType.MESH


def filter_tables(n, width, lat, pole):
    total = n * width
    band = 2 * pole
    rows = np.arange(band, dtype=np.float64)
    k = (total / 8.0) ** 2 * (2.0 + 4.0 * rows / band)
    theta = 2.0 * np.arcsinh(0.5 / np.sqrt(k))
    power = lambda d: np.exp(-theta * d)
    norm = (1.0 - power(total)) * np.sqrt(1.0 + 4.0 * k)
    wide = lambda x: np.concatenate([np.zeros(lat - band), x])
    i = range(width)
    local = [wide((power(d) + power(total - d)) / norm) for d in i]
    east = [wide(power(width - 1 - d)) for d in i]
    west = [wide(power(d)) for d in i]
    from_west = [wide(power(d + 1) / norm) for d in i]
    from_east = [wide(power(width - d) / norm) for d in i]
    inverse = [wide(1.0 / k)]
    table = np.stack(local + east + west + from_west + from_east + inverse)
    table = np.broadcast_to(table[:, None, :], (len(table), 8, lat))
    hops = np.stack(
        [
            np.concatenate([power(width * (m - 1))] * 4 + [power(width * (n - m - 1))] * 4)
            for m in range(1, n)
        ]
    )
    hops = np.broadcast_to(hops[:, None, :], (n - 1, 8, lat))
    return table.astype(np.float32), hops.astype(np.float32)


def split(a):
    high = a.astype(BF16)
    return high, (a - high.astype(F32)).astype(BF16)


def dot3(a, b, transposed=False):
    dims = (((1,), (1 if transposed else 0,)), ((), ()))
    mul = lambda x, y: lax.dot_general(x, y, dims, preferred_element_type=F32)
    return mul(a[0], b[0]) + (mul(a[0], b[1]) + mul(a[1], b[0]))


def kernel(
    n,
    rows_ref,
    state_ref,
    mask_ref,
    target_ref,
    win_ref,
    wint_ref,
    bin_ref,
    wmid_ref,
    wmidt_ref,
    bmid_ref,
    wout_ref,
    woutt_ref,
    tab_ref,
    hop_ref,
    final_ref,
    sens_ref,
    grad_ref,
    ext1,
    raw,
    ext2,
    adj,
    rim,
    upd,
    feat,
    stress,
    hid1,
    hid2,
    sendv,
    recvv,
    gsend,
    grecv,
    halo_send,
    halo_recv,
    fil_send,
    fil_recv,
    red_send,
    red_recv,
):
    width = 8
    lat = 128
    me = lax.axis_index("lon")
    left, right = lax.rem(me + n - 1, n), lax.rem(me + 1, n)
    lane = lax.broadcasted_iota(jnp.int32, (1, 1, lat), 2)
    lane2 = lax.broadcasted_iota(jnp.int32, (8, lat), 1)
    steps = n.bit_length() - 1

    barrier = pltpu.get_barrier_semaphore()

    def greet(m, carry):
        pl.semaphore_signal(
            barrier, inc=1, device_id={"lon": lax.rem(me + m, n)}, device_id_type=MESH
        )
        return carry

    lax.fori_loop(1, n, greet, 0)

    for f in range(4):
        for i in range(width):
            ext1[2 + i, f] = state_ref[f, :, i, :]
    pl.semaphore_wait(barrier, n - 1)

    def remote(src, dst, ssem, rsem, dev):
        return pltpu.make_async_remote_copy(
            src_ref=src, dst_ref=dst, send_sem=ssem, recv_sem=rsem,
            device_id={"lon": dev}, device_id_type=MESH,
        )

    def exchange(which, src_l, src_r, dst_l, dst_r):
        a = remote(src_l, dst_l, halo_send.at[which, 0], halo_recv.at[which, 0], left)
        b = remote(src_r, dst_r, halo_send.at[which, 1], halo_recv.at[which, 1], right)
        a.start()
        b.start()
        return a, b

    def halo(which, ref):
        return exchange(
            which,
            ref.at[pl.ds(2, 2)],
            ref.at[pl.ds(8, 2)],
            ref.at[pl.ds(10, 2)],
            ref.at[pl.ds(0, 2)],
        )

    def finish(pair):
        for c in pair:
            c.wait()

    first_halo = halo(0, ext1)

    polar = lane2 == rows_ref[0]
    for j in range(1, rows_ref.shape[0]):
        polar = jnp.logical_or(polar, lane2 == rows_ref[j])
    wet = jnp.broadcast_to(mask_ref[...].astype(F32), (width, 8, lat))
    cor = 0.5 + 0.5 * (lane.astype(F32) + 0.5) / lat
    local = [
        jnp.where(polar, tab_ref[d], 1.0 if d == 0 else 0.0) for d in range(width)
    ]
    inv_k = tab_ref[5 * width]

    def dy_sides(x):
        up = jnp.where(lane == lat - 1, 0.0, pltpu.roll(x, lat - 1, 2))
        down = jnp.where(lane == 0, 0.0, pltpu.roll(x, 1, 2))
        return up, down

    def dy(x):
        up, down = dy_sides(x)
        return 0.5 * (up - down)

    def dx(x):
        return 0.5 * (x[2:] - x[:-2])

    def lap(x):
        up, down = dy_sides(x[1:-1])
        return x[2:] + x[:-2] + up + down - 4.0 * x[1:-1]

    def pad(x, count=1):
        zero = jnp.zeros((count,) + x.shape[1:], F32)
        return jnp.concatenate([zero, x, zero], 0)

    def dx_t(x):
        wide = pad(x, 2)
        return -0.5 * (wide[2:] - wide[:-2])

    def lap_t(x):
        return lap(pad(x, 2))

    def filter_start(which, b):
        packed = jnp.zeros((8, lat), F32)
        for q in range(8):
            f = q % 4
            base = width if q < 4 else 2 * width
            moment = b[0][f] * tab_ref[base]
            for i in range(1, width):
                moment += b[i][f] * tab_ref[base + i]
            shift = (16 * q + 16) % lat
            packed += pltpu.roll(moment, shift, 1) if shift else moment
        sendv[which] = packed

        def push(m, carry):
            remote(
                sendv.at[which], recvv.at[which, m - 1],
                fil_send.at[which], fil_recv.at[which], lax.rem(me + m, n),
            ).start()
            return carry

        lax.fori_loop(1, n, push, 0)

    def filter_finish(which, b):
        out = []
        for i in range(width):
            cols = []
            for f in range(4):
                acc = local[i] * b[0][f]
                for j in range(1, width):
                    acc += local[abs(i - j)] * b[j][f]
                cols.append(acc)
            out.append(cols)
        whole = remote(
            recvv.at[which], recvv.at[which], fil_send.at[which], fil_recv.at[which], right
        )
        whole.wait_recv()
        whole.wait_send()
        total = jnp.sum(recvv[which] * hop_ref[...], axis=0)
        for f in range(4):
            parts = []
            for q in (f, f + 4):
                shift = (lat - 16 - 16 * q) % lat
                parts.append(pltpu.roll(total, shift, 1) if shift else total)
            for i in range(width):
                out[i][f] = out[i][f] + jnp.where(
                    polar,
                    tab_ref[3 * width + i] * parts[0] + tab_ref[4 * width + i] * parts[1],
                    0.0,
                )
        return out

    columns = width + 2
    win = win_ref[...]
    woutt = woutt_ref[...]
    bias_in = bin_ref[...]
    bias_mid = bmid_ref[...]

    def closure(step, ext):
        u, v = ext[:, 0], ext[:, 1]
        du, dv = dx(u), dx(v)
        eu, ev = dy(u[1:-1]), dy(v[1:-1])
        x = (dv - eu, eu + dv, du - ev)
        for c in range(3):
            for e in range(columns):
                feat[step, :, c, e * lat : (e + 1) * lat] = x[c][e]
        feat[step, :, 3, :] = jnp.ones((8, columns * lat), F32)
        feat[step, :, 4:8, :] = jnp.zeros((8, 4, columns * lat), F32)
        wmid = split(wmid_ref[...])
        wout = split(wout_ref[...])

        def level(l, carry):
            xl = feat[step, l]
            z = bias_in + win[:, 0:1] * xl[0:1] + win[:, 1:2] * xl[1:2] + win[:, 2:3] * xl[2:3]
            h = jnp.tanh(z)
            hid1[step, l] = h
            g = jnp.tanh(dot3(wmid, split(h)) + bias_mid)
            hid2[step, l] = g
            stress[l] = GAIN * dot3(wout, split(g))
            return carry

        lax.fori_loop(0, 8, level, 0)

    def columns_of(ref, c):
        return jnp.stack([ref[:, c, e * lat : (e + 1) * lat] for e in range(columns)])

    def update(ext):
        sxx, sxy, syy = (columns_of(stress, c) for c in range(3))
        fx = dx(sxx) + dy(sxy[1:-1])
        fy = dx(sxy) + dy(syy[1:-1])
        u, v, t, s = (ext[:, f] for f in range(4))
        cu, cv = u[2:-2], v[2:-2]
        buoy = 0.6 * t - 0.4 * s
        nu = wet * (
            cu + DT * (cor * cv - PRESS * dx(buoy[1:-1]) + fx + VISC * lap(u[1:-1]))
        )
        nv = wet * (
            cv + DT * (-cor * nu - PRESS * dy(buoy[2:-2]) + fy + VISC * lap(v[1:-1]))
        )
        upd[:, 0] = nu
        upd[:, 1] = nv
        for f, q in ((2, t), (3, s)):
            upd[:, f] = wet * (
                q[2:-2]
                + DT * (-cu * dx(q[1:-1]) - cv * dy(q[2:-2]) + VISC * lap(q[1:-1]))
            )

    def back_closure(step, gu, gv, need_state):
        hu, hv = (DT * GAIN) * gu, (DT * GAIN) * gv
        ds = (dx_t(hu), dx_t(hv) - pad(dy(hu)), -pad(dy(hv)))
        for c in range(3):
            for e in range(columns):
                stress[:, c, e * lat : (e + 1) * lat] = ds[c][e]
        stress[:, 3:8, :] = jnp.zeros((8, 5, columns * lat), F32)
        wmidt = split(wmidt_ref[...])
        wint = split(wint_ref[...])

        def level(l, carry):
            d = stress[l]
            h, g = hid1[step, l], hid2[step, l]
            xl = split(feat[step, l])
            dg = woutt[:, 0:1] * d[0:1] + woutt[:, 1:2] * d[1:2] + woutt[:, 2:3] * d[2:3]
            dz2 = split(dg * (1.0 - g * g))
            dh = dot3(wmidt, dz2)
            dz1 = split(dh * (1.0 - h * h))
            gsend[0, 0:64] += dot3(dz2, split(h), True)
            gsend[0, 64:72] += dot3(xl, dz1, True)
            gsend[0, 72:80] += dot3(xl, dz2, True)
            gsend[0, 80:88] += dot3(split(d), split(g), True)
            if need_state:
                stress[l] = dot3(wint, dz1)
            return carry

        lax.fori_loop(0, 8, level, 0)

    gsend[0] = jnp.zeros(gsend.shape[1:], F32)

    finish(first_halo)
    ext = ext1[...]
    closure(0, ext)
    update(ext)
    for i in range(width):
        raw[2 + i] = upd[i]
    second_halo = halo(1, raw)
    b = [[upd[i, f] for f in range(4)] for i in range(width)]
    filter_start(0, b)
    mid = filter_finish(0, b)
    finish(second_halo)
    for f in range(4):
        for i in range(width):
            ext2[2 + i, f] = mid[i][f]
        for edge, near, out in (((2, 3), (1, 0), 0), ((9, 8), (10, 11), 1)):
            x0, x1 = mid[edge[0] - 2][f], mid[edge[1] - 2][f]
            b0 = b[edge[0] - 2][f]
            for place in near:
                got = raw[place, f]
                fresh = jnp.where(polar, (x0 - x1) + (x0 + (x0 - b0) * inv_k), got)
                ext2[place, f] = fresh
                x1, x0, b0 = x0, fresh, got

    closure(1, ext2[...])
    update(ext2[...])
    b = [[upd[i, f] for f in range(4)] for i in range(width)]
    filter_start(1, b)
    last = filter_finish(1, b)
    scaling = 1.0 / (8 * lat * width)
    b = []
    for i in range(width):
        weight = scaling * (1.0 + 2.0 * (me * width + i).astype(F32) / (n * width))
        cols = []
        for f in range(4):
            final_ref[f, :, i, :] = last[i][f]
            cols.append(weight * (last[i][f] - target_ref[f, :, i, :]))
        b.append(cols)
    filter_start(2, b)
    a = filter_finish(2, b)
    for i in range(width):
        for f in range(4):
            upd[i, f] = a[i][f]

    gv = wet * upd[:, 1]
    gu = wet * (upd[:, 0] - DT * cor * gv)
    back_closure(1, gu, gv, True)
    ext = ext2[...]
    u, v, t, s = (ext[:, f] for f in range(4))
    cu, cv = u[2:-2], v[2:-2]
    avort, ashear, astretch = (columns_of(stress, c) for c in range(3))
    au = pad(pad(gu) + (DT * VISC) * lap_t(gu) - dy(ashear - avort)) + dx_t(astretch)
    av = (
        pad(pad(gv + DT * cor * gu) + (DT * VISC) * lap_t(gv) + dy(astretch))
        + dx_t(avort + ashear)
    )
    buoy_adj = (-DT * PRESS) * (dx_t(gu) - pad(dy(gv)))
    for f, q, gain in ((2, t, 0.6), (3, s, -0.4)):
        gq = wet * upd[:, f]
        scaled = DT * gq
        au = au - pad(scaled * dx(q[1:-1]), 2)
        av = av - pad(scaled * dy(q[2:-2]), 2)
        aq = pad(gq + dy(cv * scaled)) + VISC * lap_t(scaled) - dx_t(cu * scaled)
        adj[:, f] = pad(aq + gain * buoy_adj)
    adj[:, 0] = au
    adj[:, 1] = av
    rims = exchange(
        2, adj.at[pl.ds(0, 2)], adj.at[pl.ds(10, 2)], rim.at[1], rim.at[0]
    )
    finish(rims)
    b = []
    for i in range(width):
        cols = []
        for f in range(4):
            value = adj[2 + i, f]
            if i < 2:
                value = value + rim[0, i, f]
            if i >= width - 2:
                value = value + rim[1, i - (width - 2), f]
            sens_ref[f, :, i, :] = value * float(8 * lat * width)
            cols.append(value)
        b.append(cols)
    filter_start(3, b)
    a = filter_finish(3, b)
    for i in range(width):
        for f in range(2):
            upd[i, f] = a[i][f]
    gv = wet * upd[:, 1]
    gu = wet * (upd[:, 0] - DT * cor * gv)
    back_closure(0, gu, gv, False)

    for r in range(steps):
        stride = 1 << r
        partner = me + stride * (1 - 2 * lax.rem(me // stride, 2))
        c = remote(gsend.at[r], grecv.at[r], red_send.at[r], red_recv.at[r], partner)
        c.start()
        c.wait()
        both = gsend[r] + grecv[r]
        if r + 1 < steps:
            gsend[r + 1] = both
        else:
            grad_ref[...] = both


def on_device(
    n, ocean_state, ocean_mask, polar_rows, target_state,
    weight_in, bias_in, weight_mid, bias_mid, weight_out,
):
    width, lat = ocean_state.shape[2], ocean_state.shape[3]
    hidden = weight_in.shape[0]
    table, hops = filter_tables(n, width, lat, polar_rows.shape[0])
    steps = n.bit_length() - 1
    wide = (width + 2) * lat
    vmem = pl.BlockSpec(memory_space=pltpu.VMEM)
    smem = pl.BlockSpec(memory_space=pltpu.SMEM)
    grid = lambda *lead: pltpu.VMEM(lead + (4, 8, lat), F32)
    dma = pltpu.SemaphoreType.DMA
    final, sens, grads = pl.pallas_call(
        functools.partial(kernel, n),
        out_shape=(
            jax.ShapeDtypeStruct(ocean_state.shape, F32),
            jax.ShapeDtypeStruct(ocean_state.shape, F32),
            jax.ShapeDtypeStruct((hidden + 24, hidden), F32),
        ),
        in_specs=[smem] + [vmem] * 13,
        out_specs=[vmem] * 3,
        scratch_shapes=[
            grid(width + 4),
            grid(width + 4),
            grid(width + 4),
            grid(width + 4),
            grid(2, 2),
            grid(width),
            pltpu.VMEM((2, 8, 8, wide), F32),
            pltpu.VMEM((8, 8, wide), F32),
            pltpu.VMEM((2, 8, hidden, wide), F32),
            pltpu.VMEM((2, 8, hidden, wide), F32),
            pltpu.VMEM((4, 8, lat), F32),
            pltpu.VMEM((4, n - 1, 8, lat), F32),
            pltpu.VMEM((steps, hidden + 24, hidden), F32),
            pltpu.VMEM((steps, hidden + 24, hidden), F32),
            dma((3, 2)),
            dma((3, 2)),
            dma((4,)),
            dma((4,)),
            dma((steps,)),
            dma((steps,)),
        ],
        compiler_params=pltpu.CompilerParams(
            collective_id=0, has_side_effects=True, vmem_limit_bytes=48 * 1024 * 1024
        ),
    )(
        polar_rows,
        ocean_state,
        ocean_mask.reshape(width, 1, lat),
        target_state,
        weight_in,
        jnp.pad(weight_in.T, ((0, 5), (0, 0))),
        bias_in.reshape(hidden, 1),
        weight_mid,
        weight_mid.T,
        bias_mid.reshape(hidden, 1),
        jnp.pad(weight_out, ((0, 5), (0, 0))),
        weight_out.T,
        table,
        hops,
    )
    return (
        final,
        sens,
        grads[hidden : hidden + 3].T,
        grads[hidden + 3],
        grads[:hidden],
        grads[hidden + 11],
        grads[hidden + 16 : hidden + 19],
    )


def solution(mesh):
    field = P(None, "grp", "lon", None)
    in_specs = (field, P("lon", None), P(), field, P(), P(), P(), P(), P())
    out_specs = (field, field, P("grp", None), P("grp"), P("grp", None), P("grp"), P("grp", None))
    return jax.shard_map(
        functools.partial(on_device, mesh.shape["lon"]),
        mesh=mesh, in_specs=in_specs, out_specs=out_specs, check_vma=False,
    )
```

profile of v0, /device:TPU:0, one launch (start us, length us, event | category | flops | bytes accessed | tf_op | source)
XLA Modules:
  0.0 81.2 jit_solution(1878258075352734261)
XLA Ops:
  0.6 0.0 copy-start
  0.6 0.7 pad.7.wint_ref
  1.4 0.7 pad.8.wout_ref
  2.1 0.7 copy.21.bin_ref
  2.8 0.7 copy.22.bmid_ref
  3.5 0.8 copy.20.win_ref
  4.3 0.0 copy-start.7
  4.3 0.8 %copy.18 = f32[64,64]{0,1:T(8,128)S(1)} copy(f32[64,64]{1,0:T(8,128)} %wmid_ref.1) | data formatting | bytes 32768 | tf_op args[6]
  5.2 0.0 copy-start.3
  5.2 0.0 copy-done.7
  5.2 0.0 copy-start.5
  5.2 0.1 copy.19
  5.3 0.0 copy-start.6
  5.3 0.0 copy-done
  5.3 0.6 copy-done.3
  5.9 0.0 copy-done.5
  5.9 0.0 copy-done.6
  6.0 0.0 copy-start.1
  6.0 0.9 %copy-done.1 = f32[4,8,8,128]{3,2,1,0:T(8,128)S(1)} copy-done((f32[4,8,8,128]{3,2,1,0:T(8,128)S(1)}, f32[4,8,8,128]{3,2,1,0:T(8,128)}, u32[]{:S(2)}) %copy-start.1) | copy-done | bytes 131096
  6.9 0.0 copy-start.2
  6.9 0.9 %copy-done.2 = f32[4,8,8,128]{3,2,1,0:T(8,128)S(1)} copy-done((f32[4,8,8,128]{3,2,1,0:T(8,128)S(1)}, f32[4,8,8,128]{3,2,1,0:T(8,128)}, u32[]{:S(2)}) %copy-start.2) | copy-done | bytes 131096
  7.8 0.0 copy-start.4
  7.8 0.8 %copy-done.4 = f32[15,8,128]{2,1,0:T(8,128)S(1)} copy-done((f32[15,8,128]{2,1,0:T(8,128)S(1)}, f32[15,8,128]{2,1,0:T(8,128)}, u32[]{:S(2)}) %copy-start.4) | copy-done | bytes 61464
  8.6 69.6 %shard_map.162 = (f32[4,8,8,128]{3,2,1,0:T(8,128)S(1)}, f32[4,8,8,128]{3,2,1,0:T(8,128)S(1)}, f32[88,64]{1,0:T(8,128)S(1)}) custom-call(s32[8]{0:T(128)S(1)} %copy-done.6, f32[4,8,8,128]{3,2,1,0:T(8,128)S(1)} %copy-done.1, s32[8,1,128]{2,1,0:T(1,128)S(1)} %bitcast.14, f32[4,8,8,128]{3,2,1,0:T(8,128)S(1)} %copy-done.2, f32[64,3]{1,0:T(8,128)S(1)} %copy.20.win_ref, ...), custom_call_target="tpu_custom_call" | custom-call | tf_op jit(solution)/shard_map/pallas_call | solution.py:438
  78.2 0.5 slice_bitcast_fusion.1
  78.7 0.6 fusion
  79.3 0.6 slice.17
  79.9 0.7 copy.25
  80.6 0.7 copy.26
Async XLA Ops:
  0.6 4.7 %copy-start = (f32[41,8,128]{2,1,0:T(8,128)S(1)}, f32[41,8,128]{2,1,0:T(8,128)}, u32[]{:S(2)}) copy-start(f32[41,8,128]{2,1,0:T(8,128)} %constant.7.clone.tab_ref) | copy-start | bytes 503812
  4.3 0.9 %copy-start.7 = (f32[3,64]{1,0:T(4,128)S(1)}, f32[3,64]{1,0:T(4,128)}, u32[]{:S(2)}) copy-start(f32[3,64]{1,0:T(4,128)} %param.19) | copy-start | bytes 2308
  5.2 0.8 copy-start.3
  5.2 0.8 copy-start.5
  5.3 0.7 copy-start.6
  6.0 0.9 %copy-start.1 = (f32[4,8,8,128]{3,2,1,0:T(8,128)S(1)}, f32[4,8,8,128]{3,2,1,0:T(8,128)}, u32[]{:S(2)}) copy-start(f32[4,8,8,128]{3,2,1,0:T(8,128)} %state_ref.1) | copy-start | bytes 393220
  6.9 0.9 %copy-start.2 = (f32[4,8,8,128]{3,2,1,0:T(8,128)S(1)}, f32[4,8,8,128]{3,2,1,0:T(8,128)}, u32[]{:S(2)}) copy-start(f32[4,8,8,128]{3,2,1,0:T(8,128)} %target_ref.1) | copy-start | bytes 393220
  7.8 0.8 %copy-start.4 = (f32[15,8,128]{2,1,0:T(8,128)S(1)}, f32[15,8,128]{2,1,0:T(8,128)}, u32[]{:S(2)}) copy-start(f32[15,8,128]{2,1,0:T(8,128)} %constant.8.clone.hop_ref) | copy-start | bytes 184324
where the time goes:
time: 81.6 us; the launch traced here: 81.2 us
  Pallas kernels  69.6 us (85%)
  local copies, waits for them, and re-layouts  10.9 us (13%)
    pallas_call x1, Pallas kernels, on_device(): pl.pallas_call(functools.partial(kernel, n), out_shape=(jax.ShapeDtypeStr...  69.6 us
    unnamed x21, local copies, waits for them, and re-layouts  6.32 us

commit v1 on v0

--- a/solution.py
+++ b/solution.py
@@ -50,10 +50,29 @@
     return high, (a - high.astype(F32)).astype(BF16)
 
 
-def dot3(a, b, transposed=False):
-    dims = (((1,), (1 if transposed else 0,)), ((), ()))
-    mul = lambda x, y: lax.dot_general(x, y, dims, preferred_element_type=F32)
-    return mul(a[0], b[0]) + (mul(a[0], b[1]) + mul(a[1], b[0]))
+def left_side(a):
+    high = a.astype(BF16).astype(F32)
+    return jnp.concatenate([high, high, a - high], 1).astype(BF16)
+
+
+def dot3(a, b):
+    b = jnp.concatenate([b[0], b[1], b[0]], 0)
+    return jnp.dot(a, b, preferred_element_type=F32)
+
+
+def stacked(a):
+    high = a.astype(BF16).astype(F32)
+    return jnp.concatenate([a, a - high], 0).astype(BF16)
+
+
+def outer(a, b):
+    dims = (((1,), (1,)), ((), ()))
+    return lax.dot_general(a, b, dims, preferred_element_type=F32)
+
+
+def folded(acc, rows):
+    turned = pltpu.roll(acc, 64, 1)
+    return (acc[:rows] + (turned[:rows] + acc[rows:]))[:, :64]
 
 
 def kernel(
@@ -89,6 +108,9 @@
     recvv,
     gsend,
     grecv,
+    acc_mid,
+    acc_in,
+    acc_out,
     halo_send,
     halo_recv,
     fil_send,
@@ -250,8 +272,8 @@
                 feat[step, :, c, e * lat : (e + 1) * lat] = x[c][e]
         feat[step, :, 3, :] = jnp.ones((8, columns * lat), F32)
         feat[step, :, 4:8, :] = jnp.zeros((8, 4, columns * lat), F32)
-        wmid = split(wmid_ref[...])
-        wout = split(wout_ref[...])
+        wmid = left_side(wmid_ref[...])
+        wout = left_side(wout_ref[...])
 
         def level(l, carry):
             xl = feat[step, l]
@@ -296,28 +318,30 @@
             for e in range(columns):
                 stress[:, c, e * lat : (e + 1) * lat] = ds[c][e]
         stress[:, 3:8, :] = jnp.zeros((8, 5, columns * lat), F32)
-        wmidt = split(wmidt_ref[...])
-        wint = split(wint_ref[...])
+        wmidt = left_side(wmidt_ref[...])
+        wint = left_side(wint_ref[...])
 
         def level(l, carry):
             d = stress[l]
             h, g = hid1[step, l], hid2[step, l]
-            xl = split(feat[step, l])
+            xl = stacked(feat[step, l])
             dg = woutt[:, 0:1] * d[0:1] + woutt[:, 1:2] * d[1:2] + woutt[:, 2:3] * d[2:3]
             dz2 = split(dg * (1.0 - g * g))
             dh = dot3(wmidt, dz2)
             dz1 = split(dh * (1.0 - h * h))
-            gsend[0, 0:64] += dot3(dz2, split(h), True)
-            gsend[0, 64:72] += dot3(xl, dz1, True)
-            gsend[0, 72:80] += dot3(xl, dz2, True)
-            gsend[0, 80:88] += dot3(split(d), split(g), True)
+            two = jnp.concatenate(dz2, 0)
+            acc_mid[...] += outer(two, stacked(h))
+            acc_in[:, 0:128] += outer(xl, jnp.concatenate(dz1, 0))
+            acc_in[:, 128:256] += outer(xl, two)
+            acc_out[...] += outer(stacked(d), stacked(g))
             if need_state:
                 stress[l] = dot3(wint, dz1)
             return carry
 
         lax.fori_loop(0, 8, level, 0)
 
-    gsend[0] = jnp.zeros(gsend.shape[1:], F32)
+    for acc in (acc_mid, acc_in, acc_out):
+        acc[...] = jnp.zeros(acc.shape, F32)
 
     finish(first_halo)
     ext = ext1[...]
@@ -409,6 +433,10 @@
     gu = wet * (upd[:, 0] - DT * cor * gv)
     back_closure(0, gu, gv, False)
 
+    gsend[0, 0:64] = folded(acc_mid[...], 64)
+    gsend[0, 64:72] = folded(acc_in[:, 0:128], 8)
+    gsend[0, 72:80] = folded(acc_in[:, 128:256], 8)
+    gsend[0, 80:88] = folded(acc_out[...], 8)
     for r in range(steps):
         stride = 1 << r
         partner = me + stride * (1 - 2 * lax.rem(me // stride, 2))
@@ -459,6 +487,9 @@
             pltpu.VMEM((4, n - 1, 8, lat), F32),
             pltpu.VMEM((steps, hidden + 24, hidden), F32),
             pltpu.VMEM((steps, hidden + 24, hidden), F32),
+            pltpu.VMEM((2 * hidden, 2 * hidden), F32),
+            pltpu.VMEM((16, 4 * hidden), F32),
+            pltpu.VMEM((16, 2 * hidden), F32),
             dma((3, 2)),
             dma((3, 2)),
             dma((4,)),

time: 81.6 us -> 75.5 us (0.925)
  Pallas kernels: 69.6 us -> 63.4 us
    pallas_call x1, Pallas kernels: 69.6 us -> 63.4 us  [on_device(): pl.pallas_call(functools.partial(kernel, n), out_shape=(jax.ShapeDtypeStr...]
where the time goes in v1:
time: 75.5 us; the launch traced here: 75 us
  Pallas kernels  63.4 us (84%)
  local copies, waits for them, and re-layouts  10.9 us (14%)
    pallas_call x1, Pallas kernels, on_device(): pl.pallas_call(functools.partial(kernel, n), out_shape=(jax.ShapeDtypeStr...  63.4 us
    unnamed x21, local copies, waits for them, and re-layouts  6.32 us

profile of v1, /device:TPU:0, one launch (start us, length us, event | category | flops | bytes accessed | tf_op | source)
XLA Modules:
  0.0 75.0 jit_solution(3391380116423866253)
XLA Ops:
  0.6 0.0 copy-start
  0.6 0.7 pad.7.wint_ref
  1.4 0.7 pad.8.wout_ref
  2.1 0.7 copy.21.bin_ref
  2.8 0.7 copy.22.bmid_ref
  3.5 0.8 %copy.20.win_ref = f32[64,3]{1,0:T(8,128)S(1)} copy(f32[64,3]{0,1:T(4,128)} %param.15) | data formatting | bytes 1536 | tf_op args[4]
  4.3 0.0 copy-start.7
  4.3 0.8 %copy.18 = f32[64,64]{0,1:T(8,128)S(1)} copy(f32[64,64]{1,0:T(8,128)} %wmid_ref.1) | data formatting | bytes 32768 | tf_op args[6]
  5.2 0.0 copy-start.3
  5.2 0.0 copy-done.7
  5.2 0.0 copy-start.5
  5.2 0.1 copy.19
  5.3 0.0 copy-start.6
  5.3 0.0 copy-done
  5.3 0.6 copy-done.3
  5.9 0.0 copy-done.5
  5.9 0.0 copy-done.6
  6.0 0.0 copy-start.1
  6.0 0.9 %copy-done.1 = f32[4,8,8,128]{3,2,1,0:T(8,128)S(1)} copy-done((f32[4,8,8,128]{3,2,1,0:T(8,128)S(1)}, f32[4,8,8,128]{3,2,1,0:T(8,128)}, u32[]{:S(2)}) %copy-start.1) | copy-done | bytes 131096
  6.9 0.0 copy-start.2
  6.9 0.9 %copy-done.2 = f32[4,8,8,128]{3,2,1,0:T(8,128)S(1)} copy-done((f32[4,8,8,128]{3,2,1,0:T(8,128)S(1)}, f32[4,8,8,128]{3,2,1,0:T(8,128)}, u32[]{:S(2)}) %copy-start.2) | copy-done | bytes 131096
  7.8 0.0 copy-start.4
  7.8 0.8 %copy-done.4 = f32[15,8,128]{2,1,0:T(8,128)S(1)} copy-done((f32[15,8,128]{2,1,0:T(8,128)S(1)}, f32[15,8,128]{2,1,0:T(8,128)}, u32[]{:S(2)}) %copy-start.4) | copy-done | bytes 61464
  8.6 63.4 %shard_map.162 = (f32[4,8,8,128]{3,2,1,0:T(8,128)S(1)}, f32[4,8,8,128]{3,2,1,0:T(8,128)S(1)}, f32[88,64]{1,0:T(8,128)S(1)}) custom-call(s32[8]{0:T(128)S(1)} %copy-done.6, f32[4,8,8,128]{3,2,1,0:T(8,128)S(1)} %copy-done.1, s32[8,1,128]{2,1,0:T(1,128)S(1)} %bitcast.14, f32[4,8,8,128]{3,2,1,0:T(8,128)S(1)} %copy-done.2, f32[64,3]{1,0:T(8,128)S(1)} %copy.20.win_ref, ...), custom_call_target="tpu_custom_call" | custom-call | tf_op jit(solution)/shard_map/pallas_call | solution.py:466
  72.0 0.5 slice_bitcast_fusion.1
  72.5 0.6 fusion
  73.1 0.6 slice.17
  73.7 0.7 copy.25
  74.4 0.7 copy.26
Async XLA Ops:
  0.6 4.7 %copy-start = (f32[41,8,128]{2,1,0:T(8,128)S(1)}, f32[41,8,128]{2,1,0:T(8,128)}, u32[]{:S(2)}) copy-start(f32[41,8,128]{2,1,0:T(8,128)} %constant.7.clone.tab_ref) | copy-start | bytes 503812
  4.3 0.9 %copy-start.7 = (f32[3,64]{1,0:T(4,128)S(1)}, f32[3,64]{1,0:T(4,128)}, u32[]{:S(2)}) copy-start(f32[3,64]{1,0:T(4,128)} %param.19) | copy-start | bytes 2308
  5.2 0.8 %copy-start.3 = (f32[64,64]{1,0:T(8,128)S(1)}, f32[64,64]{1,0:T(8,128)}, u32[]{:S(2)}) copy-start(f32[64,64]{1,0:T(8,128)} %wmid_ref.1) | copy-start | bytes 49156
  5.2 0.8 %copy-start.5 = (s32[8,128]{1,0:T(8,128)S(1)}, s32[8,128]{1,0:T(8,128)}, u32[]{:S(2)}) copy-start(s32[8,128]{1,0:T(8,128)} %param.12) | copy-start | bytes 12292
  5.3 0.7 copy-start.6
  6.0 0.9 %copy-start.1 = (f32[4,8,8,128]{3,2,1,0:T(8,128)S(1)}, f32[4,8,8,128]{3,2,1,0:T(8,128)}, u32[]{:S(2)}) copy-start(f32[4,8,8,128]{3,2,1,0:T(8,128)} %state_ref.1) | copy-start | bytes 393220
  6.9 0.9 %copy-start.2 = (f32[4,8,8,128]{3,2,1,0:T(8,128)S(1)}, f32[4,8,8,128]{3,2,1,0:T(8,128)}, u32[]{:S(2)}) copy-start(f32[4,8,8,128]{3,2,1,0:T(8,128)} %target_ref.1) | copy-start | bytes 393220
  7.8 0.8 %copy-start.4 = (f32[15,8,128]{2,1,0:T(8,128)S(1)}, f32[15,8,128]{2,1,0:T(8,128)}, u32[]{:S(2)}) copy-start(f32[15,8,128]{2,1,0:T(8,128)} %constant.8.clone.hop_ref) | copy-start | bytes 184324
